TPU v7x, 512 devices: a whole 4x4x16 slice. The times are simulated.
512 devices in a mesh: dp: 8 (over y, core), row: 16 (over z_hi, x), col: 4 (over z_lo).
Axes of the slice: x: 4, y: 4, z: 16 (z_hi: 4, z_lo: 4; z = z_hi * 4 + z_lo), core: 2. Of those that a mesh axis runs over, the one named last changes fastest.
Arguments:
- activations: bfloat16 [8192, 4096], P(('dp', 'col'), 'row'), parts along dimension 0, may hold values from -6 to 6
- weight_codes: bfloat16 [4096, 14336], P('col', 'row'), may hold values from -3.75 to 3.75, as said below
- block_scales: bfloat16 [32, 112], P('col', 'row'), may hold values from 0.0039978027 to 0.039794922
- out_grad: bfloat16 [8192, 14336], P(('dp', 'col'), 'row'), parts along dimension 0, may hold values from -6 to 6
Outputs:
- projected: bfloat16 [8192, 14336], P(('dp', 'col'), 'row'), parts along dimension 0
- input_grad: bfloat16 [8192, 4096], P(('dp', 'col'), 'row'), parts along dimension 0
There are 8 independent parts, one for each index of `dp`. A program takes and returns all parts, laid end to end along the dimension named above; an argument that names none is the same for every part. Nothing has to cross between parts.
Inputs may be any that keep to these rules, and one draw needn't show every extreme that they name: `weight_codes`: every entry is an FP8 e4m3 value, plus or minus (1 + m / 8) 2^e with m in 0 to 7 and e in -2 to 1.
All inputs are finite; a program needn't handle non-finite values.
Results may differ from a plain program's by a relative error of at most 0.02.
Values may be sent and summed in bfloat16 or wider, within the bound.
A program may use at most 64 MiB of HBM per device.

v0:
```python
import jax
import jax.numpy as jnp
from jax import lax
from jax.sharding import PartitionSpec as P

QB = 128


def dequantize(weight_codes, block_scales):
    height, breadth = weight_codes.shape
    blocks = weight_codes.astype(jnp.float32).reshape(height // QB, QB, breadth // QB, QB)
    scaled = blocks * block_scales.astype(jnp.float32)[:, None, :, None]
    return scaled.reshape(height, breadth).astype(jnp.bfloat16)


def local(activations, weight_codes, block_scales, out_grad):
    full_rows = lax.all_gather(activations, "row", axis=1, tiled=True)
    tok_rows = activations.shape[0]
    col_width = weight_codes.shape[0]
    unit_width = weight_codes.shape[1]
    all_codes, all_scales = (
        lax.all_gather(weight_codes, "col", axis=0, tiled=True),
        lax.all_gather(block_scales, "col", axis=0, tiled=True),
    )
    weight = dequantize(all_codes, all_scales)
    col_blocks = all_codes.shape[0] // col_width
    col_terms = jnp.einsum(
        "tcd,cdf->ctf",
        full_rows.reshape(tok_rows, col_blocks, col_width),
        weight.reshape(col_blocks, col_width, unit_width),
        preferred_element_type=jnp.float32,
    )
    rounded = lax.optimization_barrier(col_terms.astype(jnp.bfloat16)).astype(jnp.float32)
    projected = jnp.sum(rounded, axis=0).astype(jnp.bfloat16)
    partial_value = lax.dot_general(
        out_grad, weight, (((1,), (1,)), ((), ())), preferred_element_type=jnp.float32
    )
    input_grad = lax.psum_scatter(
        partial_value.astype(jnp.bfloat16), "row", scatter_dimension=1, tiled=True
    )
    return (projected, input_grad)


def solution(mesh):
    return jax.shard_map(
        local,
        mesh=mesh,
        in_specs=(
            P(("dp", "col"), "row"),
            P("col", "row"),
            P("col", "row"),
            P(("dp", "col"), "row"),
        ),
        out_specs=(P(("dp", "col"), "row"), P(("dp", "col"), "row")),
        check_vma=False,
    )
```

profile of v0, /device:TPU:1, one launch (start us, length us, event | category | flops | bytes accessed | tf_op | source)
XLA Modules:
  0.0 388.5 jit_solution(6893712484983179786)
XLA Ops:
  7.2 0.0 copy-start
  7.2 0.0 all-gather.3.cloned.1.call-start
  7.2 3.9 copy.28
  11.1 0.0 all-gather.3.cloned.1.call-update
  11.1 0.0 all-gather.5.cloned.1.call-start
  11.2 1.7 copy.30
  12.8 0.0 all-gather.5.cloned.1.call-update
  12.9 0.0 reduce-scatter.2.cloned.1.call-start
  12.9 11.4 %all_gather.10 = bf16[32,7]{1,0:T(8,128)(2,1)S(1)} all-gather(bf16[8,7]{1,0:T(8,128)(2,1)} %param.6), channel_id=1, replica_groups=mesh['dp'=8,'row'=16,'col'=4] {'col'}, dimensions={0}, use_global_device_ids=true | all-gather | bytes 560 | tf_op jit(solution)/shard_map/all_gather | solution.py:23
  24.3 0.1 copy.29
  24.4 133.1 %all-gather.3.cloned.1.call-done = bf16[4096,896]{0,1:T(8,128)(2,1)} async-done(((bf16[1024,896]{0,1:T(8,128)(2,1)}), bf16[4096,896]{0,1:T(8,128)(2,1)}) %all-gather.3.cloned.1.call-update) | async-done | bytes 7340048 | tf_op jit(solution)/shard_map/all_gather | solution.py:22
  157.5 0.0 copy-start.1
  157.5 1.9 mul.11
  159.5 1.1 copy-done.1
  160.6 10.2 %fusion = bf16[4096,896]{0,1:T(8,128)(2,1)S(1)} fusion(f32[112,8,32,128]{3,2,1,0:T(8,128)S(1)} %bitcast.22, bf16[4096,896]{0,1:T(8,128)(2,1)S(1)} %copy-done.1), kind=kLoop, calls=%fused_computation.1 | loop fusion | flops 11010048 | bytes 29360128 | tf_op jit(solution)/shard_map/convert_element_type | solution.py:13
  170.8 0.0 copy-start.2
  170.8 2.9 copy-done.2
  173.8 0.0 copy-done
  173.8 3.8 fusion.4
  177.5 0.0 reduce-scatter.2.cloned.1.call-update
  177.6 77.5 %all-gather.5.cloned.1.call-done = bf16[256,4096]{0,1:T(8,128)(2,1)} async-done(((bf16[256,256]{0,1:T(8,128)(2,1)}), bf16[256,4096]{0,1:T(8,128)(2,1)}) %all-gather.5.cloned.1.call-update) | async-done | bytes 2097168 | tf_op jit(solution)/shard_map/all_gather | solution.py:17
  255.1 5.7 %convert_bitcast_fusion = bf16[4,256,896]{1,2,0:T(8,128)(2,1)S(1)} fusion(bf16[256,4,1024]{0,2,1:T(8,128)(2,1)} %bitcast.24, bf16[112,4,8,1024]{3,2,1,0:T(8,128)(2,1)} %bitcast.23), kind=kOutput, calls=%fused_computation.7 | convolution fusion | flops 1879965696 | bytes 11272192 | tf_op jit(solution)/shard_map/tcd,cdf->ctf/dot_general | solution.py:27
  260.8 0.5 reduce_sum.12
  261.4 1.0 copy.33
  262.3 118.0 %reduce-scatter.2.cloned.1.call-done = bf16[256,256]{0,1:T(8,128)(2,1)} async-done(((bf16[256,4096]{0,1:T(8,128)(2,1)}), bf16[256,256]{0,1:T(8,128)(2,1)}) %reduce-scatter.2.cloned.1.call-update) | async-done | bytes 131088 | tf_op jit(solution)/shard_map/reduce_scatter | solution.py:38
  380.3 1.7 copy.34
Async XLA Ops:
  7.2 166.6 %copy-start = (bf16[256,896]{1,0:T(8,128)(2,1)S(1)}, bf16[256,896]{1,0:T(8,128)(2,1)}, u32[]{:S(2)}) copy-start(bf16[256,896]{1,0:T(8,128)(2,1)} %param.7) | copy-start | bytes 1376260
  7.2 150.3 %all-gather.3.cloned.1.call-start = ((), (), s32[]{:S(2)}) async-start(), calls=%async_computation.1 | async-start | bytes 9175040 | tf_op jit(solution)/shard_map/all_gather | solution.py:22
  11.1 243.9 %all-gather.5.cloned.1.call-start = ((), (), s32[]{:S(2)}) async-start(), calls=%async_computation.2 | async-start | bytes 2228224 | tf_op jit(solution)/shard_map/all_gather | solution.py:17
  12.9 367.4 %reduce-scatter.2.cloned.1.call-start = ((), (), s32[]{:S(2)}) async-start(), calls=%async_computation.3 | async-start | bytes 2228224 | tf_op jit(solution)/shard_map/reduce_scatter | solution.py:38
  157.5 3.1 copy-start.1
  170.8 3.0 copy-start.2
Sparse Core Ops, SparseCore 0:
  11.2 146.2 all-gather.2
  161.1 93.8 all-gather.4
  259.2 121.0 reduce-scatter.1
where the time goes:
time: 389 us; the launch traced here: 388 us
  waiting for transfers between devices  329 us (85%)
  local copies, waits for them, and re-layouts  14.3 us (4%)
  between operations  13.8 us (4%)
  blocking collectives  11.4 us (3%)
  other arithmetic  10.7 us (3%)
  matrix products  9.5 us (2%)
    all_gather x1, waiting for transfers between devices, local(): lax.all_gather(weight_codes, 'col', axis=0, tiled=True)  133 us
    reduce_scatter x1, waiting for transfers between devices, local(): lax.psum_scatter(partial_value.astype(jnp.bfloat16), 'row', scatter_dimen...  118 us
    all_gather x1, waiting for transfers between devices, local(): full_rows = lax.all_gather(activations, 'row', axis=1, tiled=True)  77.5 us
    unnamed x10, local copies, waits for them, and re-layouts  12.3 us
    all_gather x1, blocking collectives, local(): lax.all_gather(block_scales, 'col', axis=0, tiled=True)  11.4 us
    convert_element_type x1, other arithmetic, dequantize(): return scaled.reshape(height, breadth).astype(jnp.bfloat16)  10.2 us
  transfers between devices with their start and end apart: 3, of which 3 were waited for; matrix products, arithmetic and copies ran while one was open for 6% of the time, Pallas kernels for 0%

commit v1 on v0

v1 whole, which is shorter than its diff:
```python
import jax
import jax.numpy as jnp
from jax import lax
from jax.experimental import pallas as pl
from jax.experimental.pallas import tpu as pltpu
from jax.sharding import PartitionSpec as P

QB = 128
F32 = jnp.float32
BF16 = jnp.bfloat16
MESH = pl.DeviceIdType.MESH


def kernel(
    act_hbm, codes_hbm, scales_ref, grad_hbm, proj_ref, igrad_ref,
    codes, grad, weight, acts, total,
    part_out, part_in_half, part_in, sums, far_out, far_in_half, far_in,
    local_sem,
    wz_send, wz_recv, wy_send, wy_recv, wc_send, wc_recv,
    az_send, az_recv, ax_send, ax_recv,
    gx_send, gx_recv, gz_send, gz_recv,
):
    dp, row, zl = lax.axis_index("dp"), lax.axis_index("row"), lax.axis_index("col")
    y, c = dp // 2, dp % 2
    zh, x = row // 4, row % 4

    def at(dy=0, dc=0, dz=0, dx=0):
        return (((y + dy) % 4) * 2 + (c + dc) % 2, ((zh + dz) % 4) * 4 + (x + dx) % 4, zl)

    LEFT, RIGHT = -1, 1
    x_at = {d: at(dx=d) for d in (LEFT, RIGHT)}
    y_at = {d: at(dy=d) for d in (LEFT, RIGHT)}
    z_at = {d: at(dz=d) for d in (LEFT, RIGHT)}
    other_core = at(dc=1)

    def line_at(col):
        return (dp, row, col)

    s_of = [
        zl,
        jnp.where(zl % 2 == 0, zl + 1, zl - 1),
        jnp.where(zl < 2, 2, 1),
        jnp.where(zl < 2, 3, 0),
    ]

    copies = []

    def remote(src, dst, ssem, rsem, dev):
        return pltpu.make_async_remote_copy(
            src_ref=src, dst_ref=dst, send_sem=ssem, recv_sem=rsem, device_id=dev, device_id_type=MESH
        )

    def send(src, dst, ssem, rsem, dev):
        copy = remote(src, dst, ssem, rsem, dev)
        copy.start()
        copies.append(copy)

    def arrived(dst, ssem, rsem):
        remote(dst, dst, ssem, rsem, other_core).wait_recv()

    load_codes = pltpu.make_async_copy(codes_hbm, codes, local_sem.at[0])
    load_act = pltpu.make_async_copy(act_hbm, acts.at[row], local_sem.at[1])
    load_grad = pltpu.make_async_copy(grad_hbm, grad, local_sem.at[2])
    load_codes.start()
    load_act.start()
    load_grad.start()

    barrier = pltpu.get_barrier_semaphore()
    for dev in (*x_at.values(), *y_at.values(), *z_at.values(), other_core):
        pl.semaphore_signal(barrier, inc=1, device_id=dev, device_id_type=MESH)

    @pl.when(zl > 0)
    def _():
        pl.semaphore_signal(barrier, inc=1, device_id=line_at(zl - 1), device_id_type=MESH)

    @pl.when(zl < 3)
    def _():
        pl.semaphore_signal(barrier, inc=1, device_id=line_at(zl + 1), device_id_type=MESH)

    def half(core):
        return pl.ds(pl.multiple_of(core * QB, QB), QB)

    mine = half(c)
    theirs = half(1 - c)
    scales = scales_ref[...].astype(F32)
    scale_row = lax.broadcasted_iota(jnp.int32, scales.shape, 0)

    def dequantize(j):
        scale = jnp.sum(jnp.where(scale_row == j, scales, 0.0), axis=0, keepdims=True)
        rows = pl.ds(pl.multiple_of(j * QB, QB), QB)
        place = zl * 4 + j // 2
        for b in range(codes.shape[1] // QB):
            cols = pl.ds(b * QB, QB)
            value = codes[rows, cols].astype(F32) * scale[:, b:b + 1]
            weight[place, half(j % 2), cols] = value.astype(BF16)

    load_codes.wait()
    dequantize(dp)
    load_act.wait()
    pl.semaphore_wait(barrier, 7 + jnp.where(zl > 0, 1, 0) + jnp.where(zl < 3, 1, 0))

    own_slice = weight.at[zl * 4 + y, mine]

    def line_copy(s, target, slot):
        w = weight.at[s * 4 + y, mine]
        return remote(w, w, wz_send.at[slot], wz_recv.at[s], line_at(target))

    @pl.when(zl < 3)
    def _():
        line_copy(zl, zl + 1, 0).start()

    @pl.when(zl > 0)
    def _():
        line_copy(zl, zl - 1, 1).start()

    first, second = pl.ds(0, 128), pl.ds(128, 128)

    def acts_z_own():
        a = acts.at[row]
        for i, d in enumerate((LEFT, RIGHT)):
            send(a, a, az_send.at[i], az_recv.at[i], z_at[d])

    def acts_z_relay():
        for i, (d, rows) in enumerate(((LEFT, second), (RIGHT, first))):
            block = acts.at[((zh - d) % 4) * 4 + x]
            arrived(block, az_send.at[i], az_recv.at[i])
            piece = block.at[rows]
            send(piece, piece, az_send.at[2 + i], az_recv.at[2 + i], z_at[d])

    def acts_z_far():
        block = acts.at[((zh + 2) % 4) * 4 + x]
        for i, rows in enumerate((second, first)):
            arrived(block.at[rows], az_send.at[2 + i], az_recv.at[2 + i])

    def acts_x_own(k):
        b = (zh + k) % 4
        a = acts.at[b * 4 + x]
        for i, d in enumerate((LEFT, RIGHT)):
            send(a, a, ax_send.at[k, i], ax_recv.at[k, i], x_at[d])

    def acts_x_relay(k):
        b = (zh + k) % 4
        for i, (d, rows) in enumerate(((LEFT, second), (RIGHT, first))):
            block = acts.at[b * 4 + (x - d) % 4]
            arrived(block, ax_send.at[k, i], ax_recv.at[k, i])
            piece = block.at[rows]
            send(piece, piece, ax_send.at[k, 2 + i], ax_recv.at[k, 2 + i], x_at[d])

    def acts_x_far(k):
        block = acts.at[((zh + k) % 4) * 4 + (x + 2) % 4]
        for i, rows in enumerate((second, first)):
            arrived(block.at[rows], ax_send.at[k, 2 + i], ax_recv.at[k, 2 + i])

    def w_line(k):
        s = s_of[k]
        w = weight.at[s * 4 + y, mine]
        arrived(w, wz_send.at[0], wz_recv.at[s])
        onward = jnp.where(s > zl, zl - 1, zl + 1)

        @pl.when((onward >= 0) & (onward <= 3))
        def _():
            line_copy(s, onward, 1 + k).start()

        for i, d in enumerate((LEFT, RIGHT)):
            send(w, w, wy_send.at[k, i], wy_recv.at[k, i], y_at[d])
        send(w, w, wc_send.at[k, 0], wc_recv.at[k, 0], other_core)

    def rows_of(i):
        return pl.ds(pl.multiple_of(c * QB + i * (QB // 2), QB // 2), QB // 2)

    def w_y_relay(k):
        s = s_of[k]
        for i, (d, h) in enumerate(((LEFT, 1), (RIGHT, 0))):
            place = s * 4 + (y - d) % 4
            w = weight.at[place, mine]
            arrived(w, wy_send.at[k, i], wy_recv.at[k, i])
            piece = weight.at[place, rows_of(h)]
            send(piece, piece, wy_send.at[k, 2 + i], wy_recv.at[k, 2 + i], y_at[d])
            send(w, w, wc_send.at[k, 1 + i], wc_recv.at[k, 1 + i], other_core)

    def w_y_far(k):
        place = s_of[k] * 4 + (y + 2) % 4
        for i, h in enumerate((1, 0)):
            arrived(weight.at[place, rows_of(h)], wy_send.at[k, 2 + i], wy_recv.at[k, 2 + i])
        w = weight.at[place, mine]
        send(w, w, wc_send.at[k, 3], wc_recv.at[k, 3], other_core)

    def w_core(k):
        s = s_of[k]
        for i, dy in enumerate((0, -LEFT, -RIGHT, 2)):
            arrived(weight.at[s * 4 + (y + dy) % 4, theirs], wc_send.at[k, i], wc_recv.at[k, i])

    def partial(k, dx):
        w = weight[s_of[k] * 4 + (x + dx) % 4]
        return lax.dot_general(grad[...], w, (((1,), (1,)), ((), ())), preferred_element_type=F32)

    def g_x_half(k):
        part_out[k, 2] = partial(k, 2).astype(BF16)
        for i, (d, rows) in enumerate(((LEFT, second), (RIGHT, first))):
            send(part_out.at[k, 2, rows], part_in_half.at[k, i], gx_send.at[k, i], gx_recv.at[k, i], x_at[d])

    def g_x_full(k):
        for i, (d, rows) in enumerate(((LEFT, second), (RIGHT, first))):
            part = partial(k, d)
            arrived(part_in_half.at[k, i], gx_send.at[k, i], gx_recv.at[k, i])
            came = part_in_half[k, i].astype(F32)
            if i == 0:
                part_out[k, i, 0:128] = part[0:128].astype(BF16)
                part_out[k, i, 128:256] = (part[128:256] + came).astype(BF16)
            else:
                part_out[k, i, 0:128] = (part[0:128] + came).astype(BF16)
                part_out[k, i, 128:256] = part[128:256].astype(BF16)
            send(part_out.at[k, i], part_in.at[k, i], gx_send.at[k, 2 + i], gx_recv.at[k, 2 + i], x_at[d])

    def far_copy(i, rows, slot):
        d = (LEFT, RIGHT)[i]
        if slot < 2:
            return remote(far_out.at[2, rows], far_in_half.at[i], gz_send.at[slot], gz_recv.at[slot], z_at[d])
        return remote(far_out.at[i], far_in.at[i], gz_send.at[slot], gz_recv.at[slot], z_at[d])

    def g_x_sum(k):
        part = partial(k, 0)
        for i in range(2):
            arrived(part_in.at[k, i], gx_send.at[k, 2 + i], gx_recv.at[k, 2 + i])
            part += part_in[k, i].astype(F32)
        away = (s_of[k] - zh) % 4

        @pl.when(away == 2)
        def _():
            far_out[2] = part.astype(BF16)
            far_copy(0, second, 0).start()
            far_copy(1, first, 1).start()

        @pl.when(away != 2)
        def _():
            sums[away] = part

    def g_z_full(k):
        away = (s_of[k] - zh) % 4

        @pl.when(away == 3)
        def _():
            arrived(far_in_half.at[0], gz_send.at[0], gz_recv.at[0])
            far_out[0, 0:128] = sums[3, 0:128].astype(BF16)
            far_out[0, 128:256] = (sums[3, 128:256] + far_in_half[0].astype(F32)).astype(BF16)
            far_copy(0, None, 2).start()

        @pl.when(away == 1)
        def _():
            arrived(far_in_half.at[1], gz_send.at[1], gz_recv.at[1])
            far_out[1, 0:128] = (sums[1, 0:128] + far_in_half[1].astype(F32)).astype(BF16)
            far_out[1, 128:256] = sums[1, 128:256].astype(BF16)
            far_copy(1, None, 3).start()

    def g_z_sum():
        part = sums[0]
        for i in range(2):
            arrived(far_in.at[i], gz_send.at[2 + i], gz_recv.at[2 + i])
            part += far_in[i].astype(F32)
        igrad_ref[...] = part.astype(BF16)

    def forward(k, start=False):
        s = s_of[k]

        @pl.loop(0, 4)
        def _(i):
            block = s * 4 + i
            term = jnp.dot(acts[block], weight[block], preferred_element_type=F32)
            if start:
                @pl.when(i == 0)
                def _():
                    total[...] = term

                @pl.when(i > 0)
                def _():
                    total[...] += term
            else:
                total[...] += term

    acts_x_own(0)
    acts_z_own()

    @pl.loop(1, 8)
    def _(step):
        dequantize((dp + step) % 8)

    load_grad.wait()
    g_x_half(0)
    w_line(1)
    g_x_full(0)
    acts_x_relay(0)
    w_line(2)
    w_y_relay(1)
    g_x_sum(0)
    acts_z_relay()
    acts_x_own(1)
    acts_x_own(3)
    acts_x_far(0)
    w_line(3)
    w_y_far(1)
    w_core(1)
    g_x_half(1)
    w_y_relay(2)
    acts_x_relay(1)
    acts_x_relay(3)
    g_z_full(0)
    g_x_full(1)
    acts_z_far()
    acts_x_own(2)
    w_y_far(2)
    w_core(2)
    g_x_half(2)
    w_y_relay(3)
    g_x_sum(1)
    acts_x_far(1)
    acts_x_far(3)
    g_x_full(2)
    g_z_full(1)
    acts_x_relay(2)
    w_y_far(3)
    w_core(3)
    g_x_half(3)
    g_x_sum(2)
    acts_x_far(2)
    forward(0, True)
    g_x_full(3)
    g_z_full(2)
    forward(1)
    g_x_sum(3)
    forward(2)
    g_z_full(3)
    forward(3)
    proj_ref[...] = total[...].astype(BF16)
    g_z_sum()

    for copy in copies:
        copy.wait_send()

    @pl.when(zl < 3)
    def _():
        line_copy(zl, zl + 1, 0).wait_send()

    @pl.when(zl > 0)
    def _():
        line_copy(zl, zl - 1, 1).wait_send()

    for k in (1, 2, 3):
        onward = jnp.where(s_of[k] > zl, zl - 1, zl + 1)

        @pl.when((onward >= 0) & (onward <= 3))
        def _():
            line_copy(s_of[k], onward, 1 + k).wait_send()

    far_copy(0, second, 0).wait_send()
    far_copy(1, first, 1).wait_send()
    far_copy(0, None, 2).wait_send()
    far_copy(1, None, 3).wait_send()


def local(activations, weight_codes, block_scales, out_grad):
    tokens, features = activations.shape
    depth, units = weight_codes.shape
    any_ref = pl.BlockSpec(memory_space=pl.ANY)
    vmem_ref = pl.BlockSpec(memory_space=pltpu.VMEM)
    dma = pltpu.SemaphoreType.DMA
    square = (tokens, features)
    half_square = (tokens // 2, features)
    return pl.pallas_call(
        kernel,
        out_shape=(
            jax.ShapeDtypeStruct((tokens, units), BF16),
            jax.ShapeDtypeStruct((tokens, features), BF16),
        ),
        in_specs=[any_ref, any_ref, vmem_ref, any_ref],
        out_specs=(vmem_ref, vmem_ref),
        scratch_shapes=[
            pltpu.VMEM((depth, units), BF16),
            pltpu.VMEM((tokens, units), BF16),
            pltpu.VMEM((16, 2 * QB, units), BF16),
            pltpu.VMEM((16, *square), BF16),
            pltpu.VMEM((tokens, units), F32),
            pltpu.VMEM((4, 3, *square), BF16),
            pltpu.VMEM((4, 2, *half_square), BF16),
            pltpu.VMEM((4, 2, *square), BF16),
            pltpu.VMEM((4, *square), F32),
            pltpu.VMEM((3, *square), BF16),
            pltpu.VMEM((2, *half_square), BF16),
            pltpu.VMEM((2, *square), BF16),
            dma((3,)),
            dma((5,)), dma((4,)),
            dma((4, 4)), dma((4, 4)),
            dma((4, 4)), dma((4, 4)),
            dma((4,)), dma((4,)),
            dma((4, 4)), dma((4, 4)),
            dma((4, 4)), dma((4, 4)),
            dma((4,)), dma((4,)),
        ],
        compiler_params=pltpu.CompilerParams(
            collective_id=0, has_side_effects=True, vmem_limit_bytes=48 * 2**20
        ),
        cost_estimate=pl.CostEstimate(
            flops=4 * tokens * 16 * features * units, bytes_accessed=4 * depth * units, transcendentals=0
        ),
        name="up_projection",
    )(activations, weight_codes, block_scales, out_grad)


def solution(mesh):
    return jax.shard_map(
        local,
        mesh=mesh,
        in_specs=(
            P(("dp", "col"), "row"),
            P("col", "row"),
            P("col", "row"),
            P(("dp", "col"), "row"),
        ),
        out_specs=(P(("dp", "col"), "row"), P(("dp", "col"), "row")),
        check_vma=False,
    )
```

time: 389 us -> 100 us (0.26)
  the two profiles are of different devices: /device:TPU:1 before, /device:TPU:120 now
where the time goes in v1:
time: 100 us
  Pallas kernels  93.9 us (94%)
  local copies, waits for them, and re-layouts  5.52 us (6%)
    pallas_call x1, Pallas kernels, local(): pl.pallas_call(kernel, out_shape=(jax.ShapeDtypeStruct((tokens, units), B...  93.9 us
    unnamed x10, local copies, waits for them, and re-layouts  5.52 us

profile of v1, /device:TPU:120, one launch (start us, length us, event | category | flops | bytes accessed | tf_op | source)
XLA Modules:
  0.0 100.1 jit_solution(8197603207320421657)
XLA Ops:
  0.6 0.0 copy-start
  0.6 1.5 %copy-done = bf16[1024,896]{1,0:T(8,128)(2,1)S(1)} copy-done((bf16[1024,896]{1,0:T(8,128)(2,1)S(1)}, bf16[1024,896]{1,0:T(8,128)(2,1)}, u32[]{:S(2)}) %copy-start) | copy-done | bytes 1835032
  2.1 0.0 copy-start.1
  2.1 1.0 %copy-done.1 = bf16[256,896]{1,0:T(8,128)(2,1)S(1)} copy-done((bf16[256,896]{1,0:T(8,128)(2,1)S(1)}, bf16[256,896]{1,0:T(8,128)(2,1)}, u32[]{:S(2)}) %copy-start.1) | copy-done | bytes 458776
  3.1 0.0 copy-start.2
  3.2 0.9 copy-done.2
  4.1 0.0 copy-start.3
  4.1 0.7 copy-done.3
  4.7 93.9 %up_projection.1 = (bf16[256,896]{1,0:T(8,128)(2,1)S(1)}, bf16[256,256]{1,0:T(8,128)(2,1)S(1)}) custom-call(bf16[256,256]{1,0:T(8,128)(2,1)S(1)} %copy-done.2, bf16[1024,896]{1,0:T(8,128)(2,1)S(1)} %copy-done, bf16[8,7]{1,0:T(8,128)(2,1)S(1)} %copy-done.3, bf16[256,896]{1,0:T(8,128)(2,1)S(1)} %copy-done.1), custom_call_target="tpu_custom_call" | custom-call | flops 3758096384 | bytes 3670016 | tf_op jit(solution)/shard_map/up_projection/pallas_call | solution.py:368
  98.7 0.8 copy.8
  99.4 0.7 copy.9
Async XLA Ops:
  0.6 1.5 %copy-start = (bf16[1024,896]{1,0:T(8,128)(2,1)S(1)}, bf16[1024,896]{1,0:T(8,128)(2,1)}, u32[]{:S(2)}) copy-start(bf16[1024,896]{1,0:T(8,128)(2,1)} %codes_hbm.1) | copy-start | bytes 5505028
  2.1 1.0 %copy-start.1 = (bf16[256,896]{1,0:T(8,128)(2,1)S(1)}, bf16[256,896]{1,0:T(8,128)(2,1)}, u32[]{:S(2)}) copy-start(bf16[256,896]{1,0:T(8,128)(2,1)} %grad_hbm.1) | copy-start | bytes 1376260
  3.1 0.9 copy-start.2
  4.1 0.7 copy-start.3

commit v2 on v0

v2 whole, which is shorter than its diff:
```python
import jax
import jax.numpy as jnp
from jax import lax
from jax.experimental import pallas as pl
from jax.experimental.pallas import tpu as pltpu
from jax.sharding import PartitionSpec as P

QB = 128
F32 = jnp.float32
BF16 = jnp.bfloat16
MESH = pl.DeviceIdType.MESH


def kernel(
    act_hbm, codes_hbm, scales_ref, grad_hbm, proj_ref, igrad_ref,
    codes, grad, weight, acts, total,
    part, part_out, part_in_half, part_in, sums, far_out, far_in_half, far_in,
    proj_out, proj_in, igrad_out, igrad_in,
    local_sem, swap_send, swap_recv,
    wz_send, wz_recv, wy_send, wy_recv,
    az_send, az_recv, ax_send, ax_recv,
    gx_send, gx_recv, gz_send, gz_recv,
):
    dp, row, zl = lax.axis_index("dp"), lax.axis_index("row"), lax.axis_index("col")
    y, c = dp // 2, dp % 2
    zh, x = row // 4, row % 4

    def at(dy=0, dc=0, dz=0, dx=0):
        return (((y + dy) % 4) * 2 + (c + dc) % 2, ((zh + dz) % 4) * 4 + (x + dx) % 4, zl)

    LEFT, RIGHT = -1, 1
    x_at = {d: at(dx=d) for d in (LEFT, RIGHT)}
    y_at = {d: at(dy=d) for d in (LEFT, RIGHT)}
    z_at = {d: at(dz=d) for d in (LEFT, RIGHT)}
    other_core = at(dc=1)

    def line_at(col):
        return (dp, row, col)

    s_of = [zl, zl + 1 - 2 * (zl % 2), (zl + 2) % 4, 3 - zl]
    inside = (zl == 1) | (zl == 2)

    copies = []

    def remote(src, dst, ssem, rsem, dev):
        return pltpu.make_async_remote_copy(
            src_ref=src, dst_ref=dst, send_sem=ssem, recv_sem=rsem, device_id=dev, device_id_type=MESH
        )

    def send(src, dst, ssem, rsem, dev):
        copy = remote(src, dst, ssem, rsem, dev)
        copy.start()
        copies.append(copy)

    def arrived(dst, ssem, rsem):
        remote(dst, dst, ssem, rsem, other_core).wait_recv()

    def tile(i, size):
        return pl.ds(pl.multiple_of(i * size, size), size)

    def half_slice(s, dy, h):
        return weight.at[s, tile((y + dy) % 4 * 2 + h, QB // 2)]

    my_tokens, their_tokens = tile(c, 256), tile(1 - c, 256)

    load_codes = [
        pltpu.make_async_copy(codes_hbm.at[tile((y + i) % 4 * 2 + c, QB)], codes.at[i], local_sem.at[i]) for i in range(4)
    ]
    load_act = pltpu.make_async_copy(
        act_hbm.at[:, tile(c, QB)], acts.at[row, my_tokens], local_sem.at[4]
    )
    load_grad = pltpu.make_async_copy(grad_hbm, grad.at[my_tokens], local_sem.at[5])
    for load in (load_codes[0], load_act, load_grad, *load_codes[1:]):
        load.start()

    barrier = pltpu.get_barrier_semaphore()
    for dev in (*x_at.values(), *y_at.values(), *z_at.values(), other_core):
        pl.semaphore_signal(barrier, inc=1, device_id=dev, device_id_type=MESH)

    @pl.when(zl > 0)
    def _():
        pl.semaphore_signal(barrier, inc=1, device_id=line_at(zl - 1), device_id_type=MESH)

    @pl.when(zl < 3)
    def _():
        pl.semaphore_signal(barrier, inc=1, device_id=line_at(zl + 1), device_id_type=MESH)

    scales = scales_ref[...].astype(F32)
    scale_row = lax.broadcasted_iota(jnp.int32, scales.shape, 0)

    def dequantize(i):
        block = (y + i) % 4
        scale = jnp.sum(jnp.where(scale_row == block * 2 + c, scales, 0.0), axis=0, keepdims=True).astype(BF16)
        load_codes[i].wait()
        for b in range(codes.shape[2] // QB):
            cols = pl.ds(b * QB, QB)
            weight[zl, tile(block, QB), cols] = codes[i, :, cols] * scale[:, b:b + 1]

    dequantize(0)
    pl.semaphore_wait(barrier, 7 + jnp.where(zl > 0, 1, 0) + jnp.where(zl < 3, 1, 0))

    their_act = act_hbm.at[:, tile(1 - c, QB)]
    send(their_act, acts.at[row, my_tokens], swap_send.at[0], swap_recv.at[0], other_core)
    send(grad_hbm, grad.at[my_tokens], swap_send.at[1], swap_recv.at[1], other_core)

    def take_act():
        load_act.wait()
        arrived(acts.at[row, their_tokens], swap_send.at[0], swap_recv.at[0])

    def take_grad():
        load_grad.wait()
        arrived(grad.at[their_tokens], swap_send.at[1], swap_recv.at[1])

    def line_copy(s, target, slot, h):
        w = half_slice(s, 0, h)
        return remote(w, w, wz_send.at[slot, h], wz_recv.at[s, h], line_at(target))

    for h in (0, 1):
        @pl.when(zl < 3)
        def _():
            line_copy(zl, zl + 1, 0, h).start()

        @pl.when(zl > 0)
        def _():
            line_copy(zl, zl - 1, 1, h).start()

    first, second = pl.ds(0, 256), pl.ds(256, 256)

    ways = ((LEFT, second, first), (RIGHT, first, second))

    def acts_piece(b, block, rows):
        return acts.at[b * 4 + block, rows]

    def acts_z_own(rest):
        for i, (d, relayed, direct) in enumerate(ways):
            piece = acts_piece(zh, x, direct if rest else relayed)
            send(piece, piece, az_send.at[4 * rest + i], az_recv.at[4 * rest + i], z_at[d])

    def acts_z_relay():
        for i, (d, relayed, _) in enumerate(ways):
            piece = acts_piece((zh - d) % 4, x, relayed)
            arrived(piece, az_send.at[i], az_recv.at[i])
            send(piece, piece, az_send.at[2 + i], az_recv.at[2 + i], z_at[d])

    def acts_z_near():
        for i, (d, _, direct) in enumerate(ways):
            arrived(acts_piece((zh - d) % 4, x, direct), az_send.at[4 + i], az_recv.at[4 + i])

    def acts_z_far():
        for i, (_, relayed, _) in enumerate(ways):
            arrived(acts_piece((zh + 2) % 4, x, relayed), az_send.at[2 + i], az_recv.at[2 + i])

    def acts_x_own(k):
        for rest in (0, 1):
            for i, (d, relayed, direct) in enumerate(ways):
                piece = acts_piece((zh + k) % 4, x, direct if rest else relayed)
                send(piece, piece, ax_send.at[k, 4 * rest + i], ax_recv.at[k, 4 * rest + i], x_at[d])

    def acts_x_relay(k):
        for i, (d, relayed, _) in enumerate(ways):
            piece = acts_piece((zh + k) % 4, (x - d) % 4, relayed)
            arrived(piece, ax_send.at[k, i], ax_recv.at[k, i])
            send(piece, piece, ax_send.at[k, 2 + i], ax_recv.at[k, 2 + i], x_at[d])

    def acts_x_far(k):
        for i, (d, relayed, direct) in enumerate(ways):
            arrived(acts_piece((zh + k) % 4, (x - d) % 4, direct), ax_send.at[k, 4 + i], ax_recv.at[k, 4 + i])
            arrived(acts_piece((zh + k) % 4, (x + 2) % 4, relayed), ax_send.at[k, 2 + i], ax_recv.at[k, 2 + i])

    def w_take(k, h):
        s = s_of[k]
        arrived(half_slice(s, 0, h), wz_send.at[0, h], wz_recv.at[s, h])
        onward = jnp.where(s > zl, zl - 1, zl + 1)

        @pl.when((onward >= 0) & (onward <= 3))
        def _():
            line_copy(s, onward, 1 + k, h).start()

    def w_take_inside(h):
        @pl.when(inside)
        def _():
            w_take(3, h)

    def w_take_end(h):
        @pl.when(jnp.logical_not(inside))
        def _():
            w_take(3, h)

    def w_y_own(k, h):
        w = half_slice(s_of[k], 0, h)
        for i, d in enumerate((LEFT, RIGHT)):
            send(w, w, wy_send.at[k, i, h], wy_recv.at[k, i, h], y_at[d])

    def w_y_relay(k):
        for i, (d, h) in enumerate(((LEFT, 1), (RIGHT, 0))):
            w = half_slice(s_of[k], -d, h)
            arrived(w, wy_send.at[k, i, h], wy_recv.at[k, i, h])
            send(w, w, wy_send.at[k, 2 + i, h], wy_recv.at[k, 2 + i, h], y_at[d])

    def w_y_rest(k):
        for i, (d, h) in enumerate(((LEFT, 0), (RIGHT, 1))):
            arrived(half_slice(s_of[k], -d, h), wy_send.at[k, i, h], wy_recv.at[k, i, h])
        for i, h in enumerate((1, 0)):
            arrived(half_slice(s_of[k], 2, h), wy_send.at[k, 2 + i, h], wy_recv.at[k, 2 + i, h])

    def span(rows):
        return slice(rows.start, rows.start + rows.size)

    def share(k, dx, rows):
        return part[k, rows, tile((x + dx) % 4, QB)]

    def g_x_first(k):
        part[k] = lax.dot_general(grad[...], weight[s_of[k]], (((1,), (1,)), ((), ())), preferred_element_type=F32)
        part_out[k, 2] = share(k, 2, slice(None)).astype(BF16)
        for i, (d, relayed, _) in enumerate(ways):
            send(part_out.at[k, 2, relayed], part_in_half.at[k, i], gx_send.at[k, i], gx_recv.at[k, i], x_at[d])
        for i, (d, _, direct) in enumerate(ways):
            part_out[k, i, direct] = share(k, d, direct).astype(BF16)
            send(part_out.at[k, i, direct], part_in.at[k, i, direct], gx_send.at[k, 4 + i], gx_recv.at[k, 4 + i], x_at[d])

    def g_x_second(k):
        for i, (d, relayed, _) in enumerate(ways):
            arrived(part_in_half.at[k, i], gx_send.at[k, i], gx_recv.at[k, i])
            part_out[k, i, relayed] = (share(k, d, relayed) + part_in_half[k, i].astype(F32)).astype(BF16)
            send(part_out.at[k, i, relayed], part_in.at[k, i, relayed], gx_send.at[k, 2 + i], gx_recv.at[k, 2 + i], x_at[d])

    def far_copy(slot):
        i = slot % 2
        d, relayed, direct = ways[i]
        if slot < 2:
            src, dst = far_out.at[2, relayed], far_in_half.at[i]
        else:
            rows = relayed if slot < 4 else direct
            src, dst = far_out.at[i, rows], far_in.at[i, rows]
        return remote(src, dst, gz_send.at[slot], gz_recv.at[slot], z_at[d])

    def g_x_sum(k):
        own = share(k, 0, slice(None))
        for i, (_, relayed, direct) in enumerate(ways):
            arrived(part_in.at[k, i, direct], gx_send.at[k, 4 + i], gx_recv.at[k, 4 + i])
            arrived(part_in.at[k, i, relayed], gx_send.at[k, 2 + i], gx_recv.at[k, 2 + i])
            own += part_in[k, i].astype(F32)
        away = (s_of[k] - zh) % 4

        @pl.when(away == 2)
        def _():
            far_out[2] = own.astype(BF16)
            far_copy(0).start()
            far_copy(1).start()

        for i, (d, relayed, direct) in enumerate(ways):
            @pl.when(away == d % 4)
            def _():
                far_out[i, direct] = own[span(direct)].astype(BF16)
                far_copy(4 + i).start()
                sums[1 + i] = own

        @pl.when(away == 0)
        def _():
            sums[0] = own

    def g_z_second(k):
        away = (s_of[k] - zh) % 4
        for i, (d, relayed, _) in enumerate(ways):
            @pl.when(away == d % 4)
            def _():
                arrived(far_in_half.at[i], gz_send.at[i], gz_recv.at[i])
                far_out[i, relayed] = (sums[1 + i, relayed] + far_in_half[i].astype(F32)).astype(BF16)
                far_copy(2 + i).start()

    def g_z_sum():
        own = sums[0]
        for i, (_, relayed, direct) in enumerate(ways):
            arrived(far_in.at[i, direct], gz_send.at[4 + i], gz_recv.at[4 + i])
            arrived(far_in.at[i, relayed], gz_send.at[2 + i], gz_recv.at[2 + i])
            own += far_in[i].astype(F32)
        sums[0] = own
        igrad_out[...] = sums[0, their_tokens].astype(BF16)
        send(igrad_out, igrad_in, swap_send.at[2], swap_recv.at[2], other_core)
        igrad_ref[:, tile(c, QB)] = sums[0, my_tokens].astype(BF16)
        arrived(igrad_in, swap_send.at[2], swap_recv.at[2])
        igrad_ref[:, tile(1 - c, QB)] = igrad_in[...]

    def forward(k):
        s = s_of[k]
        rows = jnp.concatenate([acts[s * 4 + i] for i in range(4)], axis=1)
        term = jnp.dot(rows, weight[s], preferred_element_type=F32)
        if k == 0:
            total[...] = term
        else:
            total[...] += term

    def forward_swap():
        proj_out[...] = total[their_tokens].astype(BF16)
        send(proj_out, proj_in, swap_send.at[3], swap_recv.at[3], other_core)

    def forward_sum():
        arrived(proj_in, swap_send.at[3], swap_recv.at[3])
        proj_ref[...] = (total[my_tokens] + proj_in[...].astype(F32)).astype(BF16)

    dequantize(1)
    dequantize(3)
    w_take(1, 1)
    w_take_inside(1)
    w_y_own(1, 1)
    take_grad()
    dequantize(2)
    g_x_first(0)
    w_take_inside(0)
    w_take(1, 0)
    take_act()
    w_y_own(1, 0)
    w_take(2, 1)
    w_y_own(2, 1)
    w_take(2, 0)
    acts_x_own(0)
    w_y_own(2, 0)
    w_y_relay(1)
    w_take_end(0)
    acts_x_relay(0)
    acts_z_own(0)
    w_y_own(3, 0)
    w_take_end(1)
    w_y_own(3, 1)
    g_x_second(0)
    w_y_rest(1)
    w_y_relay(2)
    g_x_first(1)
    acts_z_own(1)
    w_y_relay(3)
    g_x_second(1)
    acts_z_relay()
    w_y_rest(2)
    acts_x_far(0)
    g_x_first(2)
    g_x_sum(1)
    w_y_rest(3)
    g_x_first(3)
    acts_z_near()
    g_x_second(2)
    g_x_second(3)
    g_x_sum(0)
    acts_x_own(3)
    g_x_sum(2)
    acts_x_own(1)
    acts_z_far()
    acts_x_own(2)
    g_x_sum(3)
    acts_x_relay(3)
    acts_x_relay(1)
    g_z_second(1)
    g_z_second(2)
    g_z_second(0)
    acts_x_relay(2)
    acts_x_far(3)
    g_z_second(3)
    acts_x_far(2)
    acts_x_far(1)
    forward(0)
    forward(1)
    forward(2)
    forward(3)
    forward_swap()
    g_z_sum()
    forward_sum()

    for copy in copies:
        copy.wait_send()

    for h in (0, 1):
        @pl.when(zl < 3)
        def _():
            line_copy(zl, zl + 1, 0, h).wait_send()

        @pl.when(zl > 0)
        def _():
            line_copy(zl, zl - 1, 1, h).wait_send()

    for k in (1, 2, 3):
        onward = jnp.where(s_of[k] > zl, zl - 1, zl + 1)
        for h in (0, 1):
            @pl.when((onward >= 0) & (onward <= 3))
            def _():
                line_copy(s_of[k], onward, 1 + k, h).wait_send()

    for slot in range(6):
        far_copy(slot).wait_send()


def local(activations, weight_codes, block_scales, out_grad):
    tokens, features = activations.shape
    depth, units = weight_codes.shape
    any_ref = pl.BlockSpec(memory_space=pl.ANY)
    vmem_ref = pl.BlockSpec(memory_space=pltpu.VMEM)
    dma = pltpu.SemaphoreType.DMA
    rows = depth // 2
    share = (2 * tokens, features // 2)
    half_share = (tokens, features // 2)
    return pl.pallas_call(
        kernel,
        out_shape=(
            jax.ShapeDtypeStruct((tokens, units), BF16),
            jax.ShapeDtypeStruct((tokens, features), BF16),
        ),
        in_specs=[any_ref, any_ref, vmem_ref, any_ref],
        out_specs=(vmem_ref, vmem_ref),
        scratch_shapes=[
            pltpu.VMEM((4, QB, units), BF16),
            pltpu.VMEM((2 * tokens, units), BF16),
            pltpu.VMEM((4, rows, units), BF16),
            pltpu.VMEM((16, 2 * tokens, QB), BF16),
            pltpu.VMEM((2 * tokens, units), F32),
            pltpu.VMEM((4, 2 * tokens, rows), F32),
            pltpu.VMEM((4, 3, *share), BF16),
            pltpu.VMEM((4, 2, *half_share), BF16),
            pltpu.VMEM((4, 2, *share), BF16),
            pltpu.VMEM((3, *share), F32),
            pltpu.VMEM((3, *share), BF16),
            pltpu.VMEM((2, *half_share), BF16),
            pltpu.VMEM((2, *share), BF16),
            pltpu.VMEM((tokens, units), BF16),
            pltpu.VMEM((tokens, units), BF16),
            pltpu.VMEM(half_share, BF16),
            pltpu.VMEM(half_share, BF16),
            dma((6,)), dma((4,)), dma((4,)),
            dma((5, 2)), dma((4, 2)),
            dma((4, 4, 2)), dma((4, 4, 2)),
            dma((6,)), dma((6,)),
            dma((4, 6)), dma((4, 6)),
            dma((4, 6)), dma((4, 6)),
            dma((6,)), dma((6,)),
        ],
        compiler_params=pltpu.CompilerParams(
            collective_id=0, has_side_effects=True, vmem_limit_bytes=60 * 2**20
        ),
        cost_estimate=pl.CostEstimate(
            flops=4 * tokens * 16 * features * units, bytes_accessed=4 * depth * units, transcendentals=0
        ),
        name="up_projection",
    )(activations, weight_codes, block_scales, out_grad)


def solution(mesh):
    return jax.shard_map(
        local,
        mesh=mesh,
        in_specs=(
            P(("dp", "col"), "row"),
            P("col", "row"),
            P("col", "row"),
            P(("dp", "col"), "row"),
        ),
        out_specs=(P(("dp", "col"), "row"), P(("dp", "col"), "row")),
        check_vma=False,
    )
```

time: 389 us -> 80.3 us (0.21)
  waiting for transfers between devices: 329 us -> 0 us
  Pallas kernels: 0 us -> 75 us
  between operations: 13.8 us -> 0.64 us
  blocking collectives: 11.4 us -> 0 us
  local copies, waits for them, and re-layouts: 14.3 us -> 3.39 us
  other arithmetic: 10.7 us -> 0 us
  matrix products: 9.5 us -> 0 us
    all_gather x2 -> x0, waiting for transfers between devices: 211 us -> none  [the longest x1 133 us: local(): lax.all_gather(weight_codes, 'col', axis=0, tiled=True)]
    reduce_scatter x1 -> x0, waiting for transfers between devices: 118 us -> none  [local(): lax.psum_scatter(partial_value.astype(jnp.bfloat16), 'row', scatter_dimen...]
    pallas_call x0 -> x1, Pallas kernels: none -> 75 us  [local(): pl.pallas_call(kernel, out_shape=(jax.ShapeDtypeStruct((tokens, units), B...]
    all_gather x1 -> x0, blocking collectives: 11.4 us -> none  [local(): lax.all_gather(block_scales, 'col', axis=0, tiled=True)]
    convert_element_type x1 -> x0, other arithmetic: 10.2 us -> none  [dequantize(): return scaled.reshape(height, breadth).astype(jnp.bfloat16)]
    dot_general x2 -> x0, matrix products: 9.5 us -> none  [the longest x1 5.74 us: local(): jnp.einsum('tcd,cdf->ctf', full_rows.reshape(tok_rows, col_blocks, col_wi...]
    unnamed x10 -> x2, local copies, waits for them, and re-layouts: 12.3 us -> 3.39 us
  transfers between devices with their start and end apart: 3 -> 0, of which waited for: 3 -> 0; matrix products, arithmetic and copies ran while one was open for 6% -> 0% of each run, Pallas kernels for 0% -> 0%
where the time goes in v2:
time: 80.3 us; the launch traced here: 79 us
  Pallas kernels  75 us (93%)
  local copies, waits for them, and re-layouts  3.39 us (4%)
    pallas_call x1, Pallas kernels, local(): pl.pallas_call(kernel, out_shape=(jax.ShapeDtypeStruct((tokens, units), B...  75 us
    unnamed x2, local copies, waits for them, and re-layouts  3.39 us

profile of v2, /device:TPU:1, one launch (start us, length us, event | category | flops | bytes accessed | tf_op | source)
XLA Modules:
  0.0 79.0 jit_solution(222333098187136780)
XLA Ops:
  0.6 75.0 %up_projection.1 = (bf16[256,896]{1,0:T(8,128)(2,1)}, bf16[256,256]{1,0:T(8,128)(2,1)}) custom-call(bf16[256,256]{1,0:T(8,128)(2,1)} %act_hbm.1, bf16[1024,896]{1,0:T(8,128)(2,1)} %codes_hbm.1, bf16[8,7]{1,0:T(8,128)(2,1)} %scales_ref.1, bf16[256,896]{1,0:T(8,128)(2,1)} %grad_hbm.1), custom_call_target="tpu_custom_call" | custom-call | flops 3758096384 | bytes 3670016 | tf_op jit(solution)/shard_map/up_projection/pallas_call | solution.py:399
  75.6 1.8 %copy.8 = bf16[256,896]{1,0:T(8,128)(2,1)} copy(bf16[256,896]{1,0:T(8,128)(2,1)} %get-tuple-element.4) | data formatting | bytes 917504
  77.4 1.6 %copy.9 = bf16[256,256]{1,0:T(8,128)(2,1)} copy(bf16[256,256]{1,0:T(8,128)(2,1)} %get-tuple-element.5) | data formatting | bytes 262144

commit v3 on v2

--- a/solution.py
+++ b/solution.py
@@ -32,6 +32,7 @@
     x_at = {d: at(dx=d) for d in (LEFT, RIGHT)}
     y_at = {d: at(dy=d) for d in (LEFT, RIGHT)}
     z_at = {d: at(dz=d) for d in (LEFT, RIGHT)}
+    z_cross = {d: at(dz=d, dc=1) for d in (LEFT, RIGHT)}
     other_core = at(dc=1)
 
     def line_at(col):
@@ -74,7 +75,7 @@
         load.start()
 
     barrier = pltpu.get_barrier_semaphore()
-    for dev in (*x_at.values(), *y_at.values(), *z_at.values(), other_core):
+    for dev in (*x_at.values(), *y_at.values(), *z_at.values(), *z_cross.values(), other_core):
         pl.semaphore_signal(barrier, inc=1, device_id=dev, device_id_type=MESH)
 
     @pl.when(zl > 0)
@@ -97,7 +98,7 @@
             weight[zl, tile(block, QB), cols] = codes[i, :, cols] * scale[:, b:b + 1]
 
     dequantize(0)
-    pl.semaphore_wait(barrier, 7 + jnp.where(zl > 0, 1, 0) + jnp.where(zl < 3, 1, 0))
+    pl.semaphore_wait(barrier, 9 + jnp.where(zl > 0, 1, 0) + jnp.where(zl < 3, 1, 0))
 
     their_act = act_hbm.at[:, tile(1 - c, QB)]
     send(their_act, acts.at[row, my_tokens], swap_send.at[0], swap_recv.at[0], other_core)
@@ -228,11 +229,14 @@
         i = slot % 2
         d, relayed, direct = ways[i]
         if slot < 2:
-            src, dst = far_out.at[2, relayed], far_in_half.at[i]
-        else:
-            rows = relayed if slot < 4 else direct
-            src, dst = far_out.at[i, rows], far_in.at[i, rows]
-        return remote(src, dst, gz_send.at[slot], gz_recv.at[slot], z_at[d])
+            return remote(far_out.at[2, relayed], far_in_half.at[i], gz_send.at[slot], gz_recv.at[slot], z_at[d])
+        rows = relayed if slot < 4 else direct
+        core = rows.start // 256
+        target = (((y * 2) + core), ((zh + d) % 4) * 4 + x, zl)
+        return remote(far_out.at[i, rows], far_in.at[i, c], gz_send.at[slot], gz_recv.at[2 + 2 * i + c], target)
+
+    def igrad_copy():
+        return remote(igrad_out, igrad_in, swap_send.at[2], swap_recv.at[2], other_core)
 
     def g_x_sum(k):
         own = share(k, 0, slice(None))
@@ -258,6 +262,8 @@
         @pl.when(away == 0)
         def _():
             sums[0] = own
+            igrad_out[...] = sums[0, their_tokens].astype(BF16)
+            igrad_copy().start()
 
     def g_z_second(k):
         away = (s_of[k] - zh) % 4
@@ -269,20 +275,17 @@
                 far_copy(2 + i).start()
 
     def g_z_sum():
-        own = sums[0]
-        for i, (_, relayed, direct) in enumerate(ways):
-            arrived(far_in.at[i, direct], gz_send.at[4 + i], gz_recv.at[4 + i])
-            arrived(far_in.at[i, relayed], gz_send.at[2 + i], gz_recv.at[2 + i])
-            own += far_in[i].astype(F32)
-        sums[0] = own
-        igrad_out[...] = sums[0, their_tokens].astype(BF16)
-        send(igrad_out, igrad_in, swap_send.at[2], swap_recv.at[2], other_core)
-        igrad_ref[:, tile(c, QB)] = sums[0, my_tokens].astype(BF16)
         arrived(igrad_in, swap_send.at[2], swap_recv.at[2])
-        igrad_ref[:, tile(1 - c, QB)] = igrad_in[...]
+        parts = [sums[0, my_tokens], igrad_in[...].astype(F32)]
+        for j, core in enumerate((c, 1 - c)):
+            for i in range(2):
+                slot = 2 + 2 * i + core
+                arrived(far_in.at[i, core], gz_send.at[2], gz_recv.at[slot])
+                parts[j] += far_in[i, core].astype(F32)
+            igrad_ref[:, tile(core, QB)] = parts[j].astype(BF16)
 
     def forward(k):
-        s = s_of[k]
+        s = (zh + k) % 4
         rows = jnp.concatenate([acts[s * 4 + i] for i in range(4)], axis=1)
         term = jnp.dot(rows, weight[s], preferred_element_type=F32)
         if k == 0:
@@ -298,71 +301,71 @@
         arrived(proj_in, swap_send.at[3], swap_recv.at[3])
         proj_ref[...] = (total[my_tokens] + proj_in[...].astype(F32)).astype(BF16)
 
-    dequantize(1)
-    dequantize(3)
+    w_take_inside(1)
     w_take(1, 1)
-    w_take_inside(1)
     w_y_own(1, 1)
     take_grad()
     dequantize(2)
-    g_x_first(0)
+    dequantize(3)
+    take_act()
+    w_take(1, 0)
+    w_y_own(1, 0)
     w_take_inside(0)
-    w_take(1, 0)
-    take_act()
-    w_y_own(1, 0)
     w_take(2, 1)
     w_y_own(2, 1)
     w_take(2, 0)
+    w_y_relay(1)
+    w_y_own(2, 0)
     acts_x_own(0)
-    w_y_own(2, 0)
-    w_y_relay(1)
+    acts_x_relay(0)
+    dequantize(1)
+    w_take_end(1)
     w_take_end(0)
-    acts_x_relay(0)
+    g_x_first(0)
+    w_y_own(3, 0)
     acts_z_own(0)
-    w_y_own(3, 0)
-    w_take_end(1)
     w_y_own(3, 1)
+    w_y_rest(1)
     g_x_second(0)
-    w_y_rest(1)
+    acts_z_own(1)
     w_y_relay(2)
     g_x_first(1)
-    acts_z_own(1)
     w_y_relay(3)
     g_x_second(1)
+    w_y_rest(2)
     acts_z_relay()
-    w_y_rest(2)
-    acts_x_far(0)
     g_x_first(2)
-    g_x_sum(1)
     w_y_rest(3)
     g_x_first(3)
+    g_x_second(2)
+    g_x_sum(1)
+    g_x_second(3)
     acts_z_near()
-    g_x_second(2)
-    g_x_second(3)
     g_x_sum(0)
+    acts_z_far()
     acts_x_own(3)
     g_x_sum(2)
     acts_x_own(1)
-    acts_z_far()
+    g_x_sum(3)
+    acts_x_far(0)
     acts_x_own(2)
-    g_x_sum(3)
+    acts_x_relay(1)
+    forward(0)
+    g_z_second(0)
     acts_x_relay(3)
-    acts_x_relay(1)
+    g_z_second(2)
     g_z_second(1)
-    g_z_second(2)
-    g_z_second(0)
     acts_x_relay(2)
+    g_z_second(3)
+    acts_x_far(1)
+    forward(1)
     acts_x_far(3)
-    g_z_second(3)
+    forward(3)
     acts_x_far(2)
-    acts_x_far(1)
-    forward(0)
-    forward(1)
     forward(2)
-    forward(3)
     forward_swap()
+    forward_sum()
     g_z_sum()
-    forward_sum()
 
     for copy in copies:
         copy.wait_send()
@@ -385,6 +388,19 @@
 
     for slot in range(6):
         far_copy(slot).wait_send()
+    igrad_copy().wait_send()
+
+
+def hand_on(proj_in, igrad_in, proj_ref, igrad_ref, proj, igrad, sem):
+    loads = [pltpu.make_async_copy(proj_in, proj, sem.at[0]), pltpu.make_async_copy(igrad_in, igrad, sem.at[1])]
+    stores = [pltpu.make_async_copy(proj, proj_ref, sem.at[2]), pltpu.make_async_copy(igrad, igrad_ref, sem.at[3])]
+    for copy in loads:
+        copy.start()
+    for load, store in zip(loads, stores):
+        load.wait()
+        store.start()
+    for copy in stores:
+        copy.wait()
 
 
 def local(activations, weight_codes, block_scales, out_grad):
@@ -396,7 +412,7 @@
     rows = depth // 2
     share = (2 * tokens, features // 2)
     half_share = (tokens, features // 2)
-    return pl.pallas_call(
+    results = pl.pallas_call(
         kernel,
         out_shape=(
             jax.ShapeDtypeStruct((tokens, units), BF16),
@@ -417,7 +433,7 @@
             pltpu.VMEM((3, *share), F32),
             pltpu.VMEM((3, *share), BF16),
             pltpu.VMEM((2, *half_share), BF16),
-            pltpu.VMEM((2, *share), BF16),
+            pltpu.VMEM((2, 2, *half_share), BF16),
             pltpu.VMEM((tokens, units), BF16),
             pltpu.VMEM((tokens, units), BF16),
             pltpu.VMEM(half_share, BF16),
@@ -438,6 +454,14 @@
         ),
         name="up_projection",
     )(activations, weight_codes, block_scales, out_grad)
+    return pl.pallas_call(
+        hand_on,
+        out_shape=tuple(jax.ShapeDtypeStruct(r.shape, r.dtype) for r in results),
+        in_specs=[any_ref, any_ref],
+        out_specs=(any_ref, any_ref),
+        scratch_shapes=[*(pltpu.VMEM(r.shape, r.dtype) for r in results), dma((4,))],
+        name="hand_on",
+    )(*results)
 
 
 def solution(mesh):

time: 80.3 us -> 79.1 us (0.985)
  local copies, waits for them, and re-layouts: 3.39 us -> 0 us
  Pallas kernels: 75 us -> 77.2 us
    unnamed x2 -> x0, local copies, waits for them, and re-layouts: 3.39 us -> none
    pallas_call x0 -> x1, Pallas kernels: none -> 1.86 us  [local(): pl.pallas_call(hand_on, out_shape=tuple((jax.ShapeDtypeStruct(r.shape, r....]
where the time goes in v3:
time: 79.1 us; the launch traced here: 77.8 us
  Pallas kernels  77.2 us (98%)
    pallas_call x1, Pallas kernels, local(): pl.pallas_call(kernel, out_shape=(jax.ShapeDtypeStruct((tokens, units), B...  75.3 us
    pallas_call x1, Pallas kernels, local(): pl.pallas_call(hand_on, out_shape=tuple((jax.ShapeDtypeStruct(r.shape, r....  1.86 us

profile of v3, /device:TPU:1, one launch (start us, length us, event | category | flops | bytes accessed | tf_op | source)
XLA Modules:
  0.0 77.8 jit_solution(2445271802548852945)
XLA Ops:
  0.6 75.3 %up_projection.1 = (bf16[256,896]{1,0:T(8,128)(2,1)}, bf16[256,256]{1,0:T(8,128)(2,1)}) custom-call(bf16[256,256]{1,0:T(8,128)(2,1)} %act_hbm.1, bf16[1024,896]{1,0:T(8,128)(2,1)} %codes_hbm.1, bf16[8,7]{1,0:T(8,128)(2,1)} %scales_ref.1, bf16[256,896]{1,0:T(8,128)(2,1)} %grad_hbm.1), custom_call_target="tpu_custom_call" | custom-call | flops 3758096384 | bytes 3670016 | tf_op jit(solution)/shard_map/up_projection/pallas_call | solution.py:415
  76.0 1.9 %hand_on.1 = (bf16[256,896]{1,0:T(8,128)(2,1)}, bf16[256,256]{1,0:T(8,128)(2,1)}) custom-call(bf16[256,896]{1,0:T(8,128)(2,1)} %get-tuple-element.4.proj_in, bf16[256,256]{1,0:T(8,128)(2,1)} %get-tuple-element.5.igrad_in), custom_call_target="tpu_custom_call" | custom-call | tf_op jit(solution)/shard_map/hand_on/pallas_call | solution.py:457

commit v4 on v3

--- a/solution.py
+++ b/solution.py
@@ -100,6 +100,19 @@
     dequantize(0)
     pl.semaphore_wait(barrier, 9 + jnp.where(zl > 0, 1, 0) + jnp.where(zl < 3, 1, 0))
 
+    def line_copy(s, target, slot, h):
+        w = half_slice(s, 0, h)
+        return remote(w, w, wz_send.at[slot, h], wz_recv.at[s, h], line_at(target))
+
+    for h in (0, 1):
+        @pl.when(zl < 3)
+        def _():
+            line_copy(zl, zl + 1, 0, h).start()
+
+        @pl.when(zl > 0)
+        def _():
+            line_copy(zl, zl - 1, 1, h).start()
+
     their_act = act_hbm.at[:, tile(1 - c, QB)]
     send(their_act, acts.at[row, my_tokens], swap_send.at[0], swap_recv.at[0], other_core)
     send(grad_hbm, grad.at[my_tokens], swap_send.at[1], swap_recv.at[1], other_core)
@@ -111,19 +124,6 @@
     def take_grad():
         load_grad.wait()
         arrived(grad.at[their_tokens], swap_send.at[1], swap_recv.at[1])
-
-    def line_copy(s, target, slot, h):
-        w = half_slice(s, 0, h)
-        return remote(w, w, wz_send.at[slot, h], wz_recv.at[s, h], line_at(target))
-
-    for h in (0, 1):
-        @pl.when(zl < 3)
-        def _():
-            line_copy(zl, zl + 1, 0, h).start()
-
-        @pl.when(zl > 0)
-        def _():
-            line_copy(zl, zl - 1, 1, h).start()
 
     first, second = pl.ds(0, 256), pl.ds(256, 256)
 
@@ -301,26 +301,26 @@
         arrived(proj_in, swap_send.at[3], swap_recv.at[3])
         proj_ref[...] = (total[my_tokens] + proj_in[...].astype(F32)).astype(BF16)
 
-    w_take_inside(1)
-    w_take(1, 1)
-    w_y_own(1, 1)
+    w_take_inside(0)
+    w_take(1, 0)
+    w_y_own(1, 0)
     take_grad()
     dequantize(2)
     dequantize(3)
     take_act()
-    w_take(1, 0)
-    w_y_own(1, 0)
-    w_take_inside(0)
+    w_take(1, 1)
+    w_y_own(1, 1)
+    w_take_inside(1)
+    w_take(2, 0)
+    w_y_own(2, 0)
     w_take(2, 1)
+    w_y_relay(1)
     w_y_own(2, 1)
-    w_take(2, 0)
-    w_y_relay(1)
-    w_y_own(2, 0)
     acts_x_own(0)
     acts_x_relay(0)
     dequantize(1)
+    w_take_end(0)
     w_take_end(1)
-    w_take_end(0)
     g_x_first(0)
     w_y_own(3, 0)
     acts_z_own(0)
@@ -366,6 +366,7 @@
     forward_swap()
     forward_sum()
     g_z_sum()
+
 
     for copy in copies:
         copy.wait_send()

time: 79.1 us -> 78 us (0.986); the launches traced: 77.8 us -> 77.8 us
  no operation moved by 1% of the time
where the time goes in v4:
time: 78 us; the launch traced here: 77.8 us
  Pallas kernels  77.2 us (99%)
    pallas_call x1, Pallas kernels, local(): pl.pallas_call(kernel, out_shape=(jax.ShapeDtypeStruct((tokens, units), B...  75.3 us
    pallas_call x1, Pallas kernels, local(): pl.pallas_call(hand_on, out_shape=tuple((jax.ShapeDtypeStruct(r.shape, r....  1.86 us

profile of v4, /device:TPU:1, one launch (start us, length us, event | category | flops | bytes accessed | tf_op | source)
XLA Modules:
  0.0 77.8 jit_solution(11073276643885825588)
XLA Ops:
  0.6 75.3 %up_projection.1 = (bf16[256,896]{1,0:T(8,128)(2,1)}, bf16[256,256]{1,0:T(8,128)(2,1)}) custom-call(bf16[256,256]{1,0:T(8,128)(2,1)} %act_hbm.1, bf16[1024,896]{1,0:T(8,128)(2,1)} %codes_hbm.1, bf16[8,7]{1,0:T(8,128)(2,1)} %scales_ref.1, bf16[256,896]{1,0:T(8,128)(2,1)} %grad_hbm.1), custom_call_target="tpu_custom_call" | custom-call | flops 3758096384 | bytes 3670016 | tf_op jit(solution)/shard_map/up_projection/pallas_call | solution.py:416
  75.9 1.9 %hand_on.1 = (bf16[256,896]{1,0:T(8,128)(2,1)}, bf16[256,256]{1,0:T(8,128)(2,1)}) custom-call(bf16[256,896]{1,0:T(8,128)(2,1)} %get-tuple-element.4.proj_in, bf16[256,256]{1,0:T(8,128)(2,1)} %get-tuple-element.5.igrad_in), custom_call_target="tpu_custom_call" | custom-call | tf_op jit(solution)/shard_map/hand_on/pallas_call | solution.py:458
